TPU v7x, 32 devices: a whole 2x2x4 slice. The times are simulated.
32 devices in a mesh: dp: 8 (over y, x, core), mod: 4 (over z).
Axes of the slice: x: 2, y: 2, z: 4, core: 2. Of those that a mesh axis runs over, the one named last changes fastest.
Arguments:
- block_input: bfloat16 [2, 16384, 768], P(None, ('dp', 'mod')), may hold values from -6 to 6
- grad_out: bfloat16 [2, 16384, 768], P(None, ('dp', 'mod')), may hold values from -6 to 6
- long_flag: int32 [2, 32], P(None, ('dp', 'mod')), may hold values from 0 to 1, as said below
- valid_mask: int32 [2, 16384], P(None, ('dp', 'mod')), may hold values from 0 to 1, as said below
- labels: int32 [2, 128], P(None, ('dp', 'mod')), may hold values from 0 to 999
- tsteps: int32 [2, 128], P(None, ('dp', 'mod')), may hold values from 0 to 999
- time_table: bfloat16 [1000, 768], replicated, may hold values from -5 to 5
- class_table: bfloat16 [1000, 768], replicated, may hold values from -5 to 5
- w_ada: bfloat16 [768, 4608], P(None, 'mod'), may hold values from -0.21875 to 0.21875
- b_ada: bfloat16 [4608], P('mod'), may hold values from -3 to 3
- w_qkv: bfloat16 [768, 2304], P('mod'), may hold values from -0.21875 to 0.21875
- qv_bias: bfloat16 [1536], P('mod'), may hold values from -2 to 2
- w_proj: bfloat16 [768, 768], P('mod'), may hold values from -0.875 to 0.875
- proj_bias: bfloat16 [768], P('mod'), may hold values from -2 to 2
- w_fc1: bfloat16 [768, 3072], P('mod'), may hold values from -0.21875 to 0.21875
- fc1_bias: bfloat16 [3072], P('mod'), may hold values from -2 to 2
- w_fc2: bfloat16 [3072, 768], P('mod'), may hold values from -0.109375 to 0.109375
- fc2_bias: bfloat16 [768], P('mod'), may hold values from -2 to 2
- rel_table: bfloat16 [12, 1023], P('mod'), may hold values from -5 to 5
Outputs:
- block_output: bfloat16 [2, 16384, 768], P(None, ('dp', 'mod'))
- grad_input: bfloat16 [2, 16384, 768], P(None, ('dp', 'mod'))
- grad_time_table: float32 [1000, 768], P('mod')
- grad_class_table: float32 [1000, 768], P('mod')
- grad_w_ada: float32 [768, 4608], P(None, 'mod')
- grad_b_ada: float32 [4608], P('mod')
- grad_w_qkv: float32 [768, 2304], P('mod')
- grad_qv_bias: float32 [1536], P('mod')
- grad_w_proj: float32 [768, 768], P('mod')
- grad_proj_bias: float32 [768], P('mod')
- grad_w_fc1: float32 [768, 3072], P('mod')
- grad_fc1_bias: float32 [3072], P('mod')
- grad_w_fc2: float32 [3072, 768], P('mod')
- grad_fc2_bias: float32 [768], P('mod')
- grad_rel_table: float32 [12, 1023], P('mod')
Inputs may be any that keep to these rules, and one draw needn't show every extreme that they name: `long_flag`: 1 marks a buffer holding one sample of 512 tokens; 0 a buffer holding 4 samples of 128 tokens. `valid_mask`: each segment of 128 tokens of a buffer is valid or padding as a whole; the first segment of every buffer is valid, and all of a buffer with long_flag 1 is valid.
All inputs are finite; a program needn't handle non-finite values.
Results may differ from a plain program's by a relative error of at most 0.015.
Values may be sent and summed in bfloat16 or wider, within the bound.
No kernel may reach another device: no remote copies, remote signals or barrier semaphores. Data moves between devices by JAX's collectives and lax.ppermute only.
A program may use at most 256 MiB of HBM per device.

v0:
```python
from functools import partial
import jax
import jax.numpy as jnp
from jax import lax
from jax.sharding import PartitionSpec as P

D = 768
H = 12
HD = 64
FF = 3072
NCLS = 1000
NT = 1000
LLONG = 512
LSHORT = 128
QB = 512
MICRO = 2
SEGS = 4
HIGH = lax.Precision.HIGHEST


def norm_parts(values):
    centred = values - jnp.mean(values, axis=1, keepdims=True)
    inverse_std = lax.rsqrt(jnp.mean(centred * centred, axis=1, keepdims=True) + 1e-06)
    return (centred * inverse_std, inverse_std)


def norm_backward(grad_norm, normed, inverse_std):
    return inverse_std * (
        grad_norm
        - jnp.mean(grad_norm, axis=1, keepdims=True)
        - normed * jnp.mean(grad_norm * normed, axis=1, keepdims=True)
    )


def bias_block(table, start_row, block_rows, length):
    heads = table.shape[0]
    padded = jnp.pad(table, ((0, 0), (0, 1)))
    width = block_rows + length
    tiled = jnp.broadcast_to(padded[:, None, :], (heads, block_rows, width))
    flat = tiled.reshape(heads, block_rows * width)[:, : block_rows * (width - 1)]
    skewed = flat.reshape(heads, block_rows, width - 1)
    return skewed[:, :, block_rows - 1 : block_rows - 1 + length]


def local(
    block_input,
    grad_out,
    long_flag,
    valid_mask,
    labels,
    tsteps,
    time_table,
    class_table,
    w_ada,
    b_ada,
    w_qkv,
    qv_bias,
    w_proj,
    proj_bias,
    w_fc1,
    fc1_bias,
    w_fc2,
    fc2_bias,
    rel_table,
):
    f32 = jnp.float32
    bf16 = jnp.bfloat16
    scale = HD ** (-0.5)
    mod_count = lax.axis_size("mod")
    mod_index = lax.axis_index("mod")
    (
        full_qkv,
        full_qv_bias,
        full_proj,
        full_proj_bias,
        full_fc1,
        full_fc1_bias,
        full_fc2,
        full_fc2_bias,
        full_table,
    ) = (
        lax.all_gather(w_qkv, "mod", axis=0, tiled=True),
        lax.all_gather(qv_bias, "mod", axis=0, tiled=True),
        lax.all_gather(w_proj, "mod", axis=0, tiled=True),
        lax.all_gather(proj_bias, "mod", axis=0, tiled=True),
        lax.all_gather(w_fc1, "mod", axis=0, tiled=True),
        lax.all_gather(fc1_bias, "mod", axis=0, tiled=True),
        lax.all_gather(w_fc2, "mod", axis=0, tiled=True),
        lax.all_gather(fc2_bias, "mod", axis=0, tiled=True),
        lax.all_gather(rel_table, "mod", axis=0, tiled=True),
    )
    qkv_bias = jnp.concatenate(
        [full_qv_bias[:D].astype(f32), jnp.zeros((D,), f32), full_qv_bias[D:].astype(f32)]
    )
    table_float = full_table.astype(f32)
    ada_bias = b_ada.astype(f32)
    ada_weight = w_ada.astype(f32)
    cond = time_table[tsteps].astype(f32) + class_table[labels].astype(f32)
    act_value, silu_pull = jax.vjp(jax.nn.silu, cond)
    act_low = act_value.astype(bf16)
    grad_qkv_w = jnp.zeros(full_qkv.shape, f32)
    grad_qkv_b = jnp.zeros((3 * D,), f32)
    grad_proj_w = jnp.zeros(full_proj.shape, f32)
    grad_proj_b = jnp.zeros((D,), f32)
    grad_fc1_w = jnp.zeros(full_fc1.shape, f32)
    grad_fc1_b = jnp.zeros((FF,), f32)
    grad_fc2_w = jnp.zeros(full_fc2.shape, f32)
    grad_fc2_b = jnp.zeros((D,), f32)
    grad_table = jnp.zeros(full_table.shape, f32)
    grad_ada_w = jnp.zeros(w_ada.shape, f32)
    grad_ada_b = jnp.zeros(b_ada.shape, f32)
    outputs = []
    input_grads = []
    cond_pieces = []
    positions = jnp.arange(LLONG)
    slots = jnp.arange(SEGS)
    for micro_step in range(MICRO):
        group_act = lax.all_gather(act_low[micro_step], "mod", axis=0, tiled=True)
        columns = jnp.dot(group_act, w_ada, preferred_element_type=f32) + ada_bias
        modulation = lax.all_to_all(columns, "mod", split_axis=0, concat_axis=1, tiled=True)
        is_long = long_flag[micro_step, 0]
        owner = jnp.where(is_long > 0, 0, slots)
        select = (owner[:, None] == slots[None, :]).astype(f32)
        mod_tok = jnp.repeat(jnp.dot(select, modulation, precision=HIGH), LSHORT, axis=0)
        shift1, scale1, gate1, shift2, scale2, gate2 = jnp.split(mod_tok, 6, axis=1)
        valid_row = valid_mask[micro_step]
        valid = valid_row.astype(f32)[:, None]
        sample = jnp.where(is_long > 0, 0, positions // LSHORT)
        allowed = (sample[:, None] == sample[None, :]) & (valid_row[None, :] > 0)
        tokens = block_input[micro_step].astype(f32)
        norm1, inverse1 = norm_parts(tokens)
        entry = (norm1 * (1.0 + scale1) + shift1).astype(bf16)
        qkv_low = (jnp.dot(entry, full_qkv, preferred_element_type=f32) + qkv_bias).astype(bf16)
        query = qkv_low[:, :D].reshape(LLONG, H, HD)
        keys_all = qkv_low[:, D : 2 * D].reshape(LLONG, H, HD)
        values_all = qkv_low[:, 2 * D :].reshape(LLONG, H, HD)

        def block_probs(start):
            scores = jnp.einsum("qhd,khd->hqk", query, keys_all, preferred_element_type=f32) * scale
            scores = scores + bias_block(table_float, start, QB, LLONG)
            scores = jnp.where(allowed[None], scores, -1e30)
            top = jnp.max(scores, axis=-1, keepdims=True)
            expo = jnp.exp(scores - top)
            return expo / jnp.sum(expo, axis=-1, keepdims=True)

        block = 0
        probs = block_probs(block * QB)
        attended_parts = jnp.einsum(
            "hqk,khd->qhd", probs.astype(bf16), values_all, preferred_element_type=f32
        )
        attended = attended_parts.reshape(LLONG, D).astype(bf16)
        attn = jnp.dot(attended, full_proj, preferred_element_type=f32) + full_proj_bias.astype(f32)
        hidden = tokens + valid * gate1 * attn
        norm2, inverse2 = norm_parts(hidden)
        m_in = (norm2 * (1.0 + scale2) + shift2).astype(bf16)
        upper = jnp.dot(m_in, full_fc1, preferred_element_type=f32) + full_fc1_bias.astype(f32)
        gelu_value, gelu_pull = jax.vjp(partial(jax.nn.gelu, approximate=True), upper)
        gelu_low = gelu_value.astype(bf16)
        mlp = jnp.dot(gelu_low, full_fc2, preferred_element_type=f32) + full_fc2_bias.astype(f32)
        outputs.append((hidden + valid * gate2 * mlp).astype(bf16))
        grad_y = grad_out[micro_step].astype(f32)
        grad_mlp = (grad_y * valid * gate2).astype(bf16)
        grad_gate2 = grad_y * valid * mlp
        grad_fc2_w = grad_fc2_w + jnp.dot(gelu_low.T, grad_mlp, preferred_element_type=f32)
        grad_fc2_b = grad_fc2_b + jnp.sum(grad_mlp.astype(f32), axis=0)
        grad_gelu = jnp.einsum("td,fd->tf", grad_mlp, full_fc2, preferred_element_type=f32)
        grad_upper = gelu_pull(grad_gelu)[0].astype(bf16)
        grad_fc1_w = grad_fc1_w + jnp.dot(m_in.T, grad_upper, preferred_element_type=f32)
        grad_fc1_b = grad_fc1_b + jnp.sum(grad_upper.astype(f32), axis=0)
        grad_min = jnp.einsum("tf,df->td", grad_upper, full_fc1, preferred_element_type=f32)
        grad_scale2 = grad_min * norm2
        grad_hidden = grad_y + norm_backward(grad_min * (1.0 + scale2), norm2, inverse2)
        grad_attn = (grad_hidden * valid * gate1).astype(bf16)
        grad_gate1 = grad_hidden * valid * attn
        grad_proj_w = grad_proj_w + jnp.dot(attended.T, grad_attn, preferred_element_type=f32)
        grad_proj_b = grad_proj_b + jnp.sum(grad_attn.astype(f32), axis=0)
        grad_attended = (
            jnp.einsum("te,de->td", grad_attn, full_proj, preferred_element_type=f32)
            .astype(bf16)
            .reshape(LLONG, H, HD)
        )
        block = 0
        start = block * QB
        probs = block_probs(start)
        grad_probs = jnp.einsum(
            "qhd,khd->hqk", grad_attended, values_all, preferred_element_type=f32
        )
        delta = jnp.sum(grad_probs * probs, axis=-1, keepdims=True)
        grad_scores = (probs * (grad_probs - delta)).astype(bf16)
        grad_query_parts = (
            jnp.einsum("hqk,khd->qhd", grad_scores, keys_all, preferred_element_type=f32) * scale
        )
        grad_keys = (
            jnp.einsum("hqk,qhd->khd", grad_scores, query, preferred_element_type=f32) * scale
        )
        grad_values = jnp.einsum(
            "hqk,qhd->khd", probs.astype(bf16), grad_attended, preferred_element_type=f32
        )
        bias_value, bias_pull = jax.vjp(
            partial(bias_block, start_row=start, block_rows=QB, length=LLONG), table_float
        )
        grad_table = grad_table + bias_pull(grad_scores.astype(f32))[0]
        grad_qkv = jnp.concatenate(
            [
                grad_query_parts.reshape(LLONG, D),
                grad_keys.reshape(LLONG, D),
                grad_values.reshape(LLONG, D),
            ],
            axis=1,
        ).astype(bf16)
        grad_qkv_w = grad_qkv_w + jnp.dot(entry.T, grad_qkv, preferred_element_type=f32)
        grad_qkv_b = grad_qkv_b + jnp.sum(grad_qkv.astype(f32), axis=0)
        grad_entry = jnp.einsum("te,de->td", grad_qkv, full_qkv, preferred_element_type=f32)
        grad_scale1 = grad_entry * norm1
        input_grads.append(
            (grad_hidden + norm_backward(grad_entry * (1.0 + scale1), norm1, inverse1)).astype(bf16)
        )
        grad_mod_tok = jnp.concatenate(
            [grad_entry, grad_scale1, grad_gate1, grad_min, grad_scale2, grad_gate2], axis=1
        )
        grad_mod_seg = jnp.sum(grad_mod_tok.reshape(SEGS, LSHORT, 6 * D), axis=1)
        grad_modulation = jnp.dot(select.T, grad_mod_seg, precision=HIGH)
        grad_columns = lax.all_to_all(
            grad_modulation.astype(jnp.bfloat16), "mod", split_axis=1, concat_axis=0, tiled=True
        ).astype(grad_modulation.dtype)
        grad_ada_w = grad_ada_w + jnp.dot(group_act.astype(f32).T, grad_columns, precision=HIGH)
        grad_ada_b = grad_ada_b + jnp.sum(grad_columns, axis=0)
        cond_share = jnp.dot(grad_columns, ada_weight.T, precision=HIGH)
        cond_pieces.append(
            lax.psum_scatter(
                cond_share.astype(jnp.bfloat16), "mod", scatter_dimension=0, tiled=True
            ).astype(jnp.float32)
        )
    grad_act = jnp.stack(cond_pieces, axis=0)
    grad_cond = silu_pull(grad_act)[0].reshape(MICRO * SEGS, D)
    time_onehot = (tsteps.reshape(MICRO * SEGS)[:, None] == jnp.arange(NT)[None, :]).astype(f32)
    class_onehot = (labels.reshape(MICRO * SEGS)[:, None] == jnp.arange(NCLS)[None, :]).astype(f32)
    grad_time = jnp.dot(time_onehot.T, grad_cond, precision=HIGH)
    grad_class = jnp.dot(class_onehot.T, grad_cond, precision=HIGH)
    grad_qv = jnp.concatenate([grad_qkv_b[:D], grad_qkv_b[2 * D :]])
    summed = lax.psum(
        (
            grad_time,
            grad_class,
            grad_qkv_w,
            grad_qv,
            grad_proj_w,
            grad_proj_b,
            grad_fc1_w,
            grad_fc1_b,
            grad_fc2_w,
            grad_fc2_b,
            grad_table,
        ),
        ("dp", "mod"),
    )
    shares = tuple(
        (
            lax.dynamic_slice_in_dim(
                whole, mod_index * (whole.shape[0] // mod_count), whole.shape[0] // mod_count, 0
            )
            for whole in summed
        )
    )
    ada_w_total, ada_b_total = (
        lax.psum(grad_ada_w.astype(jnp.bfloat16), "dp").astype(jnp.float32),
        lax.psum(grad_ada_b.astype(jnp.bfloat16), "dp").astype(jnp.float32),
    )
    return (
        jnp.stack(outputs, axis=0),
        jnp.stack(input_grads, axis=0),
        shares[0],
        shares[1],
        ada_w_total,
        ada_b_total,
        shares[2],
        shares[3],
        shares[4],
        shares[5],
        shares[6],
        shares[7],
        shares[8],
        shares[9],
        shares[10],
    )


def solution(mesh):
    in_specs = (
        P(None, ("dp", "mod"), None),
        P(None, ("dp", "mod"), None),
        P(None, ("dp", "mod")),
        P(None, ("dp", "mod")),
        P(None, ("dp", "mod")),
        P(None, ("dp", "mod")),
        P(),
        P(),
        P(None, "mod"),
        P("mod"),
        P("mod", None),
        P("mod"),
        P("mod", None),
        P("mod"),
        P("mod", None),
        P("mod"),
        P("mod", None),
        P("mod"),
        P("mod", None),
    )
    out_specs = (
        P(None, ("dp", "mod"), None),
        P(None, ("dp", "mod"), None),
        P("mod", None),
        P("mod", None),
        P(None, "mod"),
        P("mod"),
        P("mod", None),
        P("mod"),
        P("mod", None),
        P("mod"),
        P("mod", None),
        P("mod"),
        P("mod", None),
        P("mod"),
        P("mod", None),
    )
    return jax.shard_map(local, mesh=mesh, in_specs=in_specs, out_specs=out_specs, check_vma=False)
```

profile of v0, /device:TPU:0, one launch (start us, length us, event | category | flops | bytes accessed | tf_op | source)
XLA Modules:
  0.0 1603.2 jit_solution(13607103833708870394)
XLA Ops:
  16.0 15.2 all-gather.1
  32.8 4.7 all-to-all-start.1
  42.9 12.5 all-reduce.12
  56.3 12.0 all-gather.2
  68.3 13.3 all-gather.3
  81.7 11.8 broadcast_in_dim.58
  93.5 11.0 pad.64
  104.5 39.7 %copy.161 = f32[2,8,512,1024]{3,1,2,0:T(8,128)} copy(f32[2,8,512,1024]{3,2,1,0:T(8,128)S(1)} %bitcast.259) | data formatting | bytes 67108864
  144.2 22.8 %slice.108 = f32[12,523776]{1,0:T(8,128)} slice(f32[12,524288]{1,0:T(8,128)} %bitcast.262), slice={[0:12], [0:523776]} | slice | bytes 50282496 | tf_op jit(solution)/shard_map/slice | solution.py:40
  166.9 54.2 %reshape.401 = f32[12,512,1023]{2,1,0:T(8,128)} reshape(f32[12,523776]{1,0:T(8,128)} %slice.108) | data formatting | bytes 50282496 | tf_op jit(solution)/shard_map/reshape | solution.py:41
  221.2 13.4 slice.109
  234.6 12.8 copy.158
  248.6 13.2 all-gather.4
  262.5 14.6 all-gather
  289.6 5.7 all-to-all-done
  302.6 4.2 fusion.17
  315.1 11.9 add_select_fusion
  327.0 15.2 fusion.146
  342.2 12.3 fusion.77
  354.5 6.0 convert_reduce_fusion.6
  364.8 7.9 fusion.149
  372.8 10.0 convert_reduce_fusion
  386.7 6.4 fusion.131
  399.2 11.5 fusion.80
  410.8 10.6 multiply_reduce_fusion
  423.9 6.9 multiply_convert_fusion
  442.0 4.3 fusion.58
  454.4 11.7 add_select_fusion.1
  466.1 15.2 fusion.147
  481.3 12.4 fusion.71
  493.6 5.8 convert_reduce_fusion.7
  502.0 5.0 fusion.148
  507.1 10.6 convert_reduce_fusion.1
  520.7 6.9 fusion.130
  535.7 12.3 fusion.74
  548.0 12.0 multiply_reduce_fusion.1
  560.0 6.9 multiply_convert_fusion.1
  573.4 5.2 fusion.151
  578.6 6.7 fusion.129
  585.4 4.9 fusion.123
  591.1 8.7 copy.160
  599.7 8.6 copy.159
  608.4 6.0 fusion.128
  633.6 4.5 bitcast_reduce_fusion.1
  639.1 8.1 convolution_add_fusion
  650.2 5.3 convolution_add_fusion.2
  655.5 8.9 convolution_add_fusion.1
  664.4 7.8 pad.40.clone
  672.1 35.2 %reshape.419 = bf16[12,523776]{1,0:T(8,128)(2,1)} reshape(bf16[12,512,1023]{2,1,0:T(8,128)(2,1)} %pad.40.clone) | data formatting | bytes 25141248 | tf_op jit(solution)/shard_map/transpose(jvp())/reshape | solution.py:41
  707.3 8.6 pad_convert_fusion
  715.9 35.8 %copy.163 = f32[2,8,512,1024]{3,2,1,0:T(8,128)} copy(f32[2,8,512,1024]{3,1,2,0:T(8,128)S(1)} %bitcast.260) | data formatting | bytes 67108864
  751.7 9.0 slice_reduce_fusion
  760.7 10.7 pad.37.clone
  771.5 34.8 %reshape.416 = bf16[12,523776]{1,0:T(8,128)(2,1)} reshape(bf16[12,512,1023]{2,1,0:T(8,128)(2,1)} %pad.37.clone) | data formatting | bytes 25141248 | tf_op jit(solution)/shard_map/transpose(jvp())/reshape | solution.py:41
  806.2 8.6 pad_convert_fusion.1
  814.8 35.9 %copy.162 = f32[2,8,512,1024]{3,2,1,0:T(8,128)} copy(f32[2,8,512,1024]{3,1,2,0:T(8,128)S(1)} %bitcast.261) | data formatting | bytes 67108864
  850.7 9.0 slice_reduce_fusion.1
  862.9 5.0 all-to-all-start.2
  868.5 5.1 all-to-all-done.2
  876.7 16.9 %all-reduce.11 = (bf16[16,768]{1,0:T(8,128)(2,1)S(1)}, bf16[16,768]{1,0:T(8,128)(2,1)S(1)}) all-reduce(bf16[16,768]{1,0:T(8,128)(2,1)S(1)} %convolution_convert_fusion.4, bf16[16,768]{1,0:T(8,128)(2,1)S(1)} %convolution_convert_fusion.5), channel_id=5, replica_groups=mesh['dp'=8,'mod'=4] {'mod'}, use_global_device_ids=true, to_apply=%region_25.26.clone | all-reduce | flops 24576 | bytes 98304
  905.0 82.4 %all-reduce.19.cloned.1.call-done = (f32[1536]{0:T(1024)}, f32[768]{0:T(1024)}, f32[3072]{0:T(1024)}, f32[768]{0:T(1024)}, f32[12,1023]{1,0:T(8,128)}) async-done(((f32[1536]{0:T(1024)}, f32[768]{0:T(1024)}, f32[3072]{0:T(1024)}, f32[768]{0:T(1024)}, f32[12,1023]{1,0:T(8,128)}), (f32[1536]{0:T(1024)}, f32[768]{0:T(1024)}, f32[3072]{0:T(1024)}, f32[768]{0:T(1024)}, ...) | async-done | bytes 73696 | tf_op jit(solution)/shard_map/psum | solution.py:241
  994.2 12.3 psum.94
  1007.2 44.8 %all-reduce.17.cloned.1.call-done = bf16[768,1152]{1,0:T(8,128)(2,1)} async-done(((bf16[768,1152]{1,0:T(8,128)(2,1)}), bf16[768,1152]{1,0:T(8,128)(2,1)}) %all-reduce.17.cloned.1.call-update) | async-done | bytes 1769488 | tf_op jit(solution)/shard_map/psum | solution.py:266
  1055.4 525.1 %all-reduce.21.cloned.1.call-done = (f32[1000,768]{1,0:T(8,128)}, f32[1000,768]{1,0:T(8,128)}, f32[768,2304]{1,0:T(8,128)}, f32[768,768]{1,0:T(8,128)}, f32[768,3072]{1,0:T(8,128)}, /*index=5*/f32[3072,768]{1,0:T(8,128)}) async-done(((f32[1000,768]{1,0:T(8,128)}, f32[1000,768]{1,0:T(8,128)}, f32[768,2304]{1,0:T(8,128)}, f32[768,768]{1,0:T(8,128)}, f32[768,3072]{1,0:T(8,128)}, ...) | async-done | bytes 34455568 | tf_op jit(solution)/shard_map/psum | solution.py:241
  (465 shorter events, 167.9 us)
Async XLA Ops:
  7.2 24.6 %copy-start = (bf16[768,1152]{1,0:T(8,128)(2,1)S(1)}, bf16[768,1152]{1,0:T(8,128)(2,1)}, u32[]{:S(2)}) copy-start(bf16[768,1152]{1,0:T(8,128)(2,1)} %param.27) | copy-start | bytes 5308420
  7.2 34.0 %copy-start.107 = (u32[32]{0:T(128)S(1)}, u32[32]{0:T(128)}, u32[]{:S(2)}) copy-start(u32[32]{0:T(128)} %constant.123) | copy-start | bytes 388
  7.2 31.6 %copy-start.112 = (s32[2,4]{1,0:T(2,128)S(1)}, s32[2,4]{1,0:T(2,128)}, u32[]{:S(2)}) copy-start(s32[2,4]{1,0:T(2,128)} %param.23) | copy-start | bytes 100
  7.2 30.9 %copy-start.111 = (s32[2,4]{1,0:T(2,128)S(1)}, s32[2,4]{1,0:T(2,128)}, u32[]{:S(2)}) copy-start(s32[2,4]{1,0:T(2,128)} %param.24) | copy-start | bytes 100
  7.2 32.2 %copy-start.109 = (s32[2,1]{0,1:T(1,128)S(1)}, s32[2,1]{0,1:T(1,128)}, u32[]{:S(2)}) copy-start(s32[2,1]{0,1:T(1,128)} %param.21) | copy-start | bytes 28
  7.2 35.2 %copy-start.116 = (bf16[192]{0:T(256)(128)(2,1)S(1)}, bf16[192]{0:T(256)(128)(2,1)}, u32[]{:S(2)}) copy-start(bf16[192]{0:T(256)(128)(2,1)} %param.32) | copy-start | bytes 1156
  7.3 35.4 %copy-start.117 = (bf16[192]{0:T(256)(128)(2,1)S(1)}, bf16[192]{0:T(256)(128)(2,1)}, u32[]{:S(2)}) copy-start(bf16[192]{0:T(256)(128)(2,1)} %param.36) | copy-start | bytes 1156
  7.3 48.1 %copy-start.8 = (bf16[2,512,768]{2,1,0:T(8,128)(2,1)S(1)}, bf16[2,512,768]{2,1,0:T(8,128)(2,1)}, u32[]{:S(2)}) copy-start(bf16[2,512,768]{2,1,0:T(8,128)(2,1)} %param.19) | copy-start | bytes 4718596
  7.3 295.3 %all-gather.10.cloned.1.call-start = ((), (), s32[]{:S(2)}) async-start(), calls=%async_computation.4 | async-start | bytes 4423680 | tf_op jit(solution)/shard_map/all_gather | solution.py:82
  8.0 346.5 %all-gather.12.cloned.1.call-start = ((), (), s32[]{:S(2)}) async-start(), calls=%async_computation.5 | async-start | bytes 1474560 | tf_op jit(solution)/shard_map/all_gather | solution.py:84
  8.8 47.5 %copy-start.110 = (bf16[384]{0:T(512)(128)(2,1)S(1)}, bf16[384]{0:T(512)(128)(2,1)}, u32[]{:S(2)}) copy-start(bf16[384]{0:T(512)(128)(2,1)} %param.30) | copy-start | bytes 2308
  8.8 59.5 %copy-start.102 = (bf16[3,1023]{1,0:T(4,128)(2,1)S(1)}, bf16[3,1023]{1,0:T(4,128)(2,1)}, u32[]{:S(2)}) copy-start(bf16[3,1023]{1,0:T(4,128)(2,1)} %param.37) | copy-start | bytes 18418
  8.8 356.1 %all-gather.14.cloned.1.call-start = ((), (), s32[]{:S(2)}) async-start(), calls=%async_computation.6 | async-start | bytes 5898240 | tf_op jit(solution)/shard_map/all_gather | solution.py:86
  32.8 251.4 %all-to-all-start.1 = ((f32[4,4,1152]{2,1,0:T(4,128)}), f32[4,4,1152]{2,1,0:T(4,128)S(1)}, u32[]{:S(2)}, u32[]{:S(2)}) async-start(f32[4,4,1152]{2,1,0:T(4,128)} %all_to_all.60), calls=%async_computation.1 | async-start | bytes 147456 | tf_op jit(solution)/shard_map/all_to_all | solution.py:120
  37.5 335.2 %all-gather.16.cloned.1.call-start = ((), (), s32[]{:S(2)}) async-start(), calls=%async_computation.7 | async-start | bytes 5898240 | tf_op jit(solution)/shard_map/all_gather | solution.py:88
  234.6 13.5 copy-start.95
  234.6 14.0 copy-start.108
  234.6 45.4 %copy-start.101 = (f32[512]{0:T(512)S(1)}, f32[512]{0:T(512)}, u32[]{:S(2)}) copy-start(f32[512]{0:T(512)} %get-tuple-element.24) | copy-start | bytes 6148
  262.5 20.8 %copy-start.106 = (pred[512]{0:T(512)(128)(4,1)S(1)}, pred[512]{0:T(512)(128)(4,1)}, u32[]{:S(2)}) copy-start(pred[512]{0:T(512)(128)(4,1)} %get-tuple-element.28) | copy-start | bytes 1540
  281.6 111.5 %copy-start.87 = (f32[1,512]{1,0:T(1,128)}, f32[1,512]{1,0:T(1,128)S(1)}, u32[]{:S(2)}) copy-start(f32[1,512]{1,0:T(1,128)S(1)} %get-tuple-element.89) | copy-start | bytes 6148
  284.2 13.4 copy-start.104
  284.2 11.1 all-to-all-start
  360.5 32.6 %copy-start.84 = (f32[512]{0:T(512)}, f32[512]{0:T(512)S(1)}, u32[]{:S(2)}) copy-start(f32[512]{0:T(512)S(1)} %broadcast_multiply_fusion.8) | copy-start | bytes 6148
  361.7 31.5 %copy-start.89 = (f32[512]{0:T(512)}, f32[512]{0:T(512)S(1)}, u32[]{:S(2)}) copy-start(f32[512]{0:T(512)S(1)} %add_rsqrt_fusion) | copy-start | bytes 6148
  364.8 17.9 %slice-start.3 = ((s8[9437184]{0:T(1024)(128)(4,1)}), s8[1048576]{0:T(1024)(128)(4,1)S(1)}, s32[]{:S(2)}) async-start(s8[9437184]{0:T(1024)(128)(4,1)} %bitcast.279), calls=%async_computation.14 | async-start | bytes 2097152
  399.2 11.5 copy-start.74
  410.7 23.8 %copy-start.51 = (bf16[12,64,512]{2,1,0:T(8,128)(2,1)}, bf16[12,64,512]{2,1,0:T(8,128)(2,1)S(1)}, u32[]{:S(2)}) copy-start(bf16[12,64,512]{2,1,0:T(8,128)(2,1)S(1)} %fusion.80) | copy-start | bytes 2359300
  410.7 10.6 slice-start.6
  410.8 11.9 slice-start.7
  410.8 13.1 slice-start.8
  452.7 13.4 copy-start.33
  454.4 11.7 copy-start.23
  481.2 12.4 copy-start.86
  502.0 15.7 slice-start
  502.0 15.7 slice-start.17
  507.0 13.7 copy-start.42
  507.0 10.6 slice-start.1
  507.1 10.6 slice-start.2
  507.1 10.6 slice-start.18
  548.0 12.0 slice-start.9
  548.0 12.0 slice-start.10
  548.0 12.0 slice-start.11
  569.5 20.7 %copy-start.68 = (bf16[12,64,512]{2,1,0:T(8,128)(2,1)}, bf16[12,64,512]{2,1,0:T(8,128)(2,1)S(1)}, u32[]{:S(2)}) copy-start(bf16[12,64,512]{2,1,0:T(8,128)(2,1)S(1)} %multiply_convert_fusion.7) | copy-start | bytes 2359300
  571.2 19.1 %copy-start.40 = (bf16[12,64,512]{2,1,0:T(8,128)(2,1)}, bf16[12,64,512]{2,1,0:T(8,128)(2,1)S(1)}, u32[]{:S(2)}) copy-start(bf16[12,64,512]{2,1,0:T(8,128)(2,1)S(1)} %multiply_convert_fusion.8) | copy-start | bytes 2359300
  608.4 11.2 slice-start.19
  608.4 11.2 slice-start.20
  630.0 232.8 %all-to-all-start.3 = ((bf16[4,4,1152]{2,0,1:T(4,128)(2,1)}), bf16[4,4,1152]{2,0,1:T(4,128)(2,1)S(1)}, u32[]{:S(2)}, u32[]{:S(2)}) async-start(bf16[4,4,1152]{2,0,1:T(4,128)(2,1)} %bitcast.52), calls=%async_computation.3 | async-start | bytes 73728 | tf_op jit(solution)/shard_map/all_to_all | solution.py:223
  633.3 354.1 %all-reduce.19.cloned.1.call-start = ((), (), s32[]{:S(2)}) async-start(), calls=%async_computation.9 | async-start | bytes 188416 | tf_op jit(solution)/shard_map/psum | solution.py:241
  633.6 15.8 slice-start.12
  639.1 10.4 slice-start.13
  650.2 14.2 slice-start.15
  850.7 10.9 copy-start.99
  850.7 10.9 copy-start.100
  850.7 11.5 copy-start.91
  850.7 11.5 copy-start.93
  850.7 22.9 %copy-start.79 = (bf16[1,16,768]{2,0,1:T(2,128)(2,1)S(1)}, bf16[1,16,768]{2,0,1:T(2,128)(2,1)}, u32[]{:S(2)}) copy-start(bf16[1,16,768]{2,0,1:T(2,128)(2,1)} %copy-done.78) | copy-start | bytes 73732
  859.8 14.5 copy-start.77
  862.9 10.7 all-to-all-start.2
  867.9 184.1 %all-reduce.17.cloned.1.call-start = ((), (), s32[]{:S(2)}) async-start(), calls=%async_computation.8 | async-start | bytes 3538944 | tf_op jit(solution)/shard_map/psum | solution.py:266
  876.1 17.7 %copy-start.81 = (bf16[8,768]{1,0:T(8,128)(2,1)S(1)}, bf16[8,768]{1,0:T(8,128)(2,1)}, u32[]{:S(2)}) copy-start(bf16[8,768]{1,0:T(8,128)(2,1)} %copy-done.80) | copy-start | bytes 36868
  876.1 17.7 %copy-start.83 = (bf16[8,768]{1,0:T(8,128)(2,1)S(1)}, bf16[8,768]{1,0:T(8,128)(2,1)}, u32[]{:S(2)}) copy-start(bf16[8,768]{1,0:T(8,128)(2,1)} %copy-done.82) | copy-start | bytes 36868
  876.1 17.7 %copy-start.114 = (s32[8]{0:T(128)S(1)}, s32[8]{0:T(128)}, u32[]{:S(2)}) copy-start(s32[8]{0:T(128)} %eq.102) | copy-start | bytes 100
  876.1 20.9 %copy-start.113 = (s32[8]{0:T(128)S(1)}, s32[8]{0:T(128)}, u32[]{:S(2)}) copy-start(s32[8]{0:T(128)} %eq.106) | copy-start | bytes 100
  893.7 686.9 %all-reduce.21.cloned.1.call-start = ((), (), s32[]{:S(2)}) async-start(), calls=%async_computation.10 | async-start | bytes 68911104 | tf_op jit(solution)/shard_map/psum | solution.py:241
  (91 other events, 408.3 us)
Sparse Core Ops, SparseCore 0:
  9.7 75.3 all-gather.9
  86.7 29.2 all-gather.11
  117.5 88.5 all-gather.13
  207.5 90.2 all-gather.15
  863.0 124.3 all-reduce.18
  991.1 60.8 all-reduce.16
  1060.1 520.4 all-reduce.20
where the time goes:
time: 1610 us; the launch traced here: 1600 us
  waiting for transfers between devices  666 us (41%)
  local copies, waits for them, and re-layouts  422 us (26%)
  matrix products  242 us (15%)
  other arithmetic  127 us (8%)
  blocking collectives  110 us (7%)
  between operations  18.9 us (1%)
  starting transfers between devices  17.2 us (1%)
    psum x2, waiting for transfers between devices, local(): lax.psum((grad_time, grad_class, grad_qkv_w, grad_qv, grad_proj_w, grad_p...  607 us
    unnamed x305, local copies, waits for them, and re-layouts  182 us
    reshape x3, local copies, waits for them, and re-layouts, bias_block(): skewed = flat.reshape(heads, block_rows, width - 1)  124 us
    psum x1, waiting for transfers between devices, local(): lax.psum(grad_ada_w.astype(jnp.bfloat16), 'dp').astype(jnp.float32)  44.8 us
  transfers between devices with their start and end apart: 11, of which 5 were waited for; matrix products, arithmetic and copies ran while one was open for 32% of the time, Pallas kernels for 0%

commit v1 on v0

--- a/solution.py
+++ b/solution.py
@@ -239,20 +239,23 @@
     grad_class = jnp.dot(class_onehot.T, grad_cond, precision=HIGH)
     grad_qv = jnp.concatenate([grad_qkv_b[:D], grad_qkv_b[2 * D :]])
     summed = lax.psum(
-        (
-            grad_time,
-            grad_class,
-            grad_qkv_w,
-            grad_qv,
-            grad_proj_w,
-            grad_proj_b,
-            grad_fc1_w,
-            grad_fc1_b,
-            grad_fc2_w,
-            grad_fc2_b,
-            grad_table,
+        lax.psum(
+            (
+                grad_time,
+                grad_class,
+                grad_qkv_w,
+                grad_qv,
+                grad_proj_w,
+                grad_proj_b,
+                grad_fc1_w,
+                grad_fc1_b,
+                grad_fc2_w,
+                grad_fc2_b,
+                grad_table,
+            ),
+            "mod",
         ),
-        ("dp", "mod"),
+        "dp",
     )
     shares = tuple(
         (

time: 1610 us -> 2620 us (1.63)
  waiting for transfers between devices: 666 us -> 1660 us
    psum x2, waiting for transfers between devices: 607 us -> 1140 us  [local(): lax.psum((grad_time, grad_class, grad_qkv_w, grad_qv, grad_proj_w, grad_p...]
    psum x0 -> x2, waiting for transfers between devices: none -> 451 us  [local(): lax.psum(lax.psum((grad_time, grad_class, grad_qkv_w, grad_qv, grad_proj_...]
  transfers between devices with their start and end apart: 11 -> 13, of which waited for: 5 -> 6; matrix products, arithmetic and copies ran while one was open for 32% -> 20% of each run, Pallas kernels for 0% -> 0%
where the time goes in v1:
time: 2620 us; the launch traced here: 2610 us
  waiting for transfers between devices  1660 us (63%)
  local copies, waits for them, and re-layouts  423 us (16%)
  matrix products  246 us (9%)
  other arithmetic  127 us (5%)
  blocking collectives  112 us (4%)
    psum x2, waiting for transfers between devices, local(): lax.psum((grad_time, grad_class, grad_qkv_w, grad_qv, grad_proj_w, grad_p...  1140 us
    psum x2, waiting for transfers between devices, local(): lax.psum(lax.psum((grad_time, grad_class, grad_qkv_w, grad_qv, grad_proj_...  451 us
    unnamed x305, local copies, waits for them, and re-layouts  183 us
    reshape x3, local copies, waits for them, and re-layouts, bias_block(): skewed = flat.reshape(heads, block_rows, width - 1)  124 us
    psum x1, waiting for transfers between devices, local(): lax.psum(grad_ada_w.astype(jnp.bfloat16), 'dp').astype(jnp.float32)  57.5 us
  transfers between devices with their start and end apart: 13, of which 6 were waited for; matrix products, arithmetic and copies ran while one was open for 20% of the time, Pallas kernels for 0%

profile of v1, /device:TPU:0, one launch (start us, length us, event | category | flops | bytes accessed | tf_op | source)
XLA Modules:
  0.0 2606.1 jit_solution(14699535161216014240)
XLA Ops:
  16.0 15.2 all-gather.1
  32.8 4.7 all-to-all-start.1
  42.9 12.5 all-reduce.14
  56.3 12.0 all-gather.2
  68.3 13.3 all-gather.3
  81.7 11.8 broadcast_in_dim.58
  93.5 11.0 pad.64
  104.5 39.7 %copy.161 = f32[2,8,512,1024]{3,1,2,0:T(8,128)} copy(f32[2,8,512,1024]{3,2,1,0:T(8,128)S(1)} %bitcast.259) | data formatting | bytes 67108864
  144.2 22.7 slice.108
  166.9 54.3 %reshape.401 = f32[12,512,1023]{2,1,0:T(8,128)} reshape(f32[12,523776]{1,0:T(8,128)} %slice.108) | data formatting | bytes 50282496 | tf_op jit(solution)/shard_map/reshape | solution.py:41
  221.2 13.4 slice.109
  234.6 12.8 copy.158
  248.7 13.2 all-gather.4
  262.5 14.6 all-gather
  289.7 5.5 all-to-all-done
  315.1 11.9 add_select_fusion
  326.9 15.2 fusion.146
  342.1 12.3 fusion.77
  354.4 6.0 convert_reduce_fusion.6
  364.7 7.9 fusion.149
  372.7 9.8 convert_reduce_fusion
  386.4 6.4 fusion.131
  399.0 11.5 fusion.80
  410.6 10.6 multiply_reduce_fusion
  423.6 6.9 multiply_convert_fusion
  441.7 4.3 fusion.58
  454.1 11.7 add_select_fusion.1
  465.8 15.2 fusion.147
  480.9 12.3 fusion.71
  493.3 5.7 convert_reduce_fusion.7
  501.6 5.0 fusion.148
  506.7 10.6 convert_reduce_fusion.1
  520.4 6.9 fusion.130
  535.3 12.3 fusion.74
  547.7 12.0 multiply_reduce_fusion.1
  559.7 6.9 multiply_convert_fusion.1
  573.0 5.2 fusion.151
  578.2 6.7 fusion.129
  585.0 4.9 fusion.123
  590.7 8.7 copy.160
  599.4 8.7 copy.159
  608.1 6.0 fusion.128
  633.3 4.5 bitcast_reduce_fusion.1
  638.7 8.1 convolution_add_fusion
  649.9 5.3 convolution_add_fusion.2
  655.2 8.9 convolution_add_fusion.1
  664.1 7.8 pad.40.clone
  671.9 35.2 %reshape.419 = bf16[12,523776]{1,0:T(8,128)(2,1)} reshape(bf16[12,512,1023]{2,1,0:T(8,128)(2,1)} %pad.40.clone) | data formatting | bytes 25141248 | tf_op jit(solution)/shard_map/transpose(jvp())/reshape | solution.py:41
  707.1 8.6 pad_convert_fusion
  715.6 35.8 %copy.163 = f32[2,8,512,1024]{3,2,1,0:T(8,128)} copy(f32[2,8,512,1024]{3,1,2,0:T(8,128)S(1)} %bitcast.260) | data formatting | bytes 67108864
  751.5 9.0 slice_reduce_fusion
  760.5 10.7 pad.37.clone
  771.2 34.8 %reshape.416 = bf16[12,523776]{1,0:T(8,128)(2,1)} reshape(bf16[12,512,1023]{2,1,0:T(8,128)(2,1)} %pad.37.clone) | data formatting | bytes 25141248 | tf_op jit(solution)/shard_map/transpose(jvp())/reshape | solution.py:41
  806.0 8.6 pad_convert_fusion.1
  814.6 35.9 %copy.162 = f32[2,8,512,1024]{3,2,1,0:T(8,128)} copy(f32[2,8,512,1024]{3,1,2,0:T(8,128)S(1)} %bitcast.261) | data formatting | bytes 67108864
  850.5 9.0 slice_reduce_fusion.1
  862.6 5.0 all-to-all-start.2
  868.3 5.2 all-to-all-done.2
  874.0 17.4 all-reduce.13
  905.2 1140.1 %all-reduce.29.cloned.1.call-done = (f32[1000,768]{1,0:T(8,128)}, f32[1000,768]{1,0:T(8,128)}, f32[768,2304]{1,0:T(8,128)}, f32[768,768]{1,0:T(8,128)}, f32[768,3072]{1,0:T(8,128)}, /*index=5*/f32[3072,768]{1,0:T(8,128)}) async-done(((f32[1000,768]{1,0:T(8,128)}, f32[1000,768]{1,0:T(8,128)}, f32[768,2304]{1,0:T(8,128)}, f32[768,768]{1,0:T(8,128)}, f32[768,3072]{1,0:T(8,128)}, ...) | async-done | bytes 34455568 | tf_op jit(solution)/shard_map/psum | solution.py:242
  2050.2 13.7 psum.173
  2064.5 36.6 %all-reduce.23.cloned.1.call-done = (f32[1536]{0:T(1024)}, f32[768]{0:T(1024)}, f32[3072]{0:T(1024)}, f32[768]{0:T(1024)}, f32[12,1023]{1,0:T(8,128)}) async-done(((f32[1536]{0:T(1024)}, f32[768]{0:T(1024)}, f32[3072]{0:T(1024)}, f32[768]{0:T(1024)}, f32[12,1023]{1,0:T(8,128)}), (f32[1536]{0:T(1024)}, f32[768]{0:T(1024)}, f32[3072]{0:T(1024)}, f32[768]{0:T(1024)}, ...) | async-done | bytes 73696 | tf_op jit(solution)/shard_map/psum | solution.py:241
  2107.9 57.5 %all-reduce.21.cloned.1.call-done = bf16[768,1152]{1,0:T(8,128)(2,1)} async-done(((bf16[768,1152]{1,0:T(8,128)(2,1)}), bf16[768,1152]{1,0:T(8,128)(2,1)}) %all-reduce.21.cloned.1.call-update) | async-done | bytes 1769488 | tf_op jit(solution)/shard_map/psum | solution.py:269
  2169.0 414.8 %all-reduce.25.cloned.1.call-done = (f32[1000,768]{1,0:T(8,128)}, f32[1000,768]{1,0:T(8,128)}, f32[768,2304]{1,0:T(8,128)}, f32[768,768]{1,0:T(8,128)}, f32[768,3072]{1,0:T(8,128)}, /*index=5*/f32[3072,768]{1,0:T(8,128)}) async-done(((f32[1000,768]{1,0:T(8,128)}, f32[1000,768]{1,0:T(8,128)}, f32[768,2304]{1,0:T(8,128)}, f32[768,768]{1,0:T(8,128)}, f32[768,3072]{1,0:T(8,128)}, ...) | async-done | bytes 34455568 | tf_op jit(solution)/shard_map/psum | solution.py:241
  (471 shorter events, 176.7 us)
Async XLA Ops:
  7.2 24.6 copy-start
  7.2 34.0 %copy-start.107 = (u32[32]{0:T(128)S(1)}, u32[32]{0:T(128)}, u32[]{:S(2)}) copy-start(u32[32]{0:T(128)} %constant.123) | copy-start | bytes 388
  7.2 31.6 %copy-start.112 = (s32[2,4]{1,0:T(2,128)S(1)}, s32[2,4]{1,0:T(2,128)}, u32[]{:S(2)}) copy-start(s32[2,4]{1,0:T(2,128)} %param.23) | copy-start | bytes 100
  7.2 30.9 %copy-start.111 = (s32[2,4]{1,0:T(2,128)S(1)}, s32[2,4]{1,0:T(2,128)}, u32[]{:S(2)}) copy-start(s32[2,4]{1,0:T(2,128)} %param.24) | copy-start | bytes 100
  7.2 32.2 %copy-start.109 = (s32[2,1]{0,1:T(1,128)S(1)}, s32[2,1]{0,1:T(1,128)}, u32[]{:S(2)}) copy-start(s32[2,1]{0,1:T(1,128)} %param.21) | copy-start | bytes 28
  7.2 35.2 %copy-start.116 = (bf16[192]{0:T(256)(128)(2,1)S(1)}, bf16[192]{0:T(256)(128)(2,1)}, u32[]{:S(2)}) copy-start(bf16[192]{0:T(256)(128)(2,1)} %param.32) | copy-start | bytes 1156
  7.3 35.4 %copy-start.117 = (bf16[192]{0:T(256)(128)(2,1)S(1)}, bf16[192]{0:T(256)(128)(2,1)}, u32[]{:S(2)}) copy-start(bf16[192]{0:T(256)(128)(2,1)} %param.36) | copy-start | bytes 1156
  7.3 48.1 %copy-start.8 = (bf16[2,512,768]{2,1,0:T(8,128)(2,1)S(1)}, bf16[2,512,768]{2,1,0:T(8,128)(2,1)}, u32[]{:S(2)}) copy-start(bf16[2,512,768]{2,1,0:T(8,128)(2,1)} %param.19) | copy-start | bytes 4718596
  7.3 295.2 %all-gather.10.cloned.1.call-start = ((), (), s32[]{:S(2)}) async-start(), calls=%async_computation.4 | async-start | bytes 4423680 | tf_op jit(solution)/shard_map/all_gather | solution.py:82
  8.0 346.4 %all-gather.12.cloned.1.call-start = ((), (), s32[]{:S(2)}) async-start(), calls=%async_computation.5 | async-start | bytes 1474560 | tf_op jit(solution)/shard_map/all_gather | solution.py:84
  8.8 47.5 %copy-start.110 = (bf16[384]{0:T(512)(128)(2,1)S(1)}, bf16[384]{0:T(512)(128)(2,1)}, u32[]{:S(2)}) copy-start(bf16[384]{0:T(512)(128)(2,1)} %param.30) | copy-start | bytes 2308
  8.8 59.5 %copy-start.102 = (bf16[3,1023]{1,0:T(4,128)(2,1)S(1)}, bf16[3,1023]{1,0:T(4,128)(2,1)}, u32[]{:S(2)}) copy-start(bf16[3,1023]{1,0:T(4,128)(2,1)} %param.37) | copy-start | bytes 18418
  8.8 355.9 %all-gather.14.cloned.1.call-start = ((), (), s32[]{:S(2)}) async-start(), calls=%async_computation.6 | async-start | bytes 5898240 | tf_op jit(solution)/shard_map/all_gather | solution.py:86
  32.8 251.4 %all-to-all-start.1 = ((f32[4,4,1152]{2,1,0:T(4,128)}), f32[4,4,1152]{2,1,0:T(4,128)S(1)}, u32[]{:S(2)}, u32[]{:S(2)}) async-start(f32[4,4,1152]{2,1,0:T(4,128)} %all_to_all.60), calls=%async_computation.1 | async-start | bytes 147456 | tf_op jit(solution)/shard_map/all_to_all | solution.py:120
  37.5 335.1 %all-gather.16.cloned.1.call-start = ((), (), s32[]{:S(2)}) async-start(), calls=%async_computation.7 | async-start | bytes 5898240 | tf_op jit(solution)/shard_map/all_gather | solution.py:88
  234.6 13.5 copy-start.95
  234.6 14.0 copy-start.108
  234.6 45.4 %copy-start.101 = (f32[512]{0:T(512)S(1)}, f32[512]{0:T(512)}, u32[]{:S(2)}) copy-start(f32[512]{0:T(512)} %get-tuple-element.24) | copy-start | bytes 6148
  262.5 20.8 copy-start.106
  281.6 111.2 %copy-start.87 = (f32[1,512]{1,0:T(1,128)}, f32[1,512]{1,0:T(1,128)S(1)}, u32[]{:S(2)}) copy-start(f32[1,512]{1,0:T(1,128)S(1)} %get-tuple-element.100) | copy-start | bytes 6148
  284.2 13.3 copy-start.104
  284.2 11.0 all-to-all-start
  360.4 32.5 %copy-start.84 = (f32[512]{0:T(512)}, f32[512]{0:T(512)S(1)}, u32[]{:S(2)}) copy-start(f32[512]{0:T(512)S(1)} %broadcast_multiply_fusion.8) | copy-start | bytes 6148
  361.5 31.4 %copy-start.89 = (f32[512]{0:T(512)}, f32[512]{0:T(512)S(1)}, u32[]{:S(2)}) copy-start(f32[512]{0:T(512)S(1)} %add_rsqrt_fusion) | copy-start | bytes 6148
  364.7 17.8 slice-start.3
  399.0 11.5 copy-start.74
  410.5 23.8 copy-start.51
  410.5 10.6 slice-start.6
  410.6 11.9 slice-start.7
  410.6 13.1 slice-start.8
  452.4 13.4 copy-start.33
  454.1 11.7 copy-start.23
  480.9 12.4 copy-start.86
  501.6 15.7 slice-start
  501.6 15.7 slice-start.17
  506.6 13.7 copy-start.42
  506.7 10.7 slice-start.1
  506.7 10.6 slice-start.2
  506.7 10.6 slice-start.18
  547.7 12.0 slice-start.9
  547.7 12.0 slice-start.10
  547.7 12.0 slice-start.11
  569.2 20.7 copy-start.68
  570.8 19.1 copy-start.40
  608.1 11.2 slice-start.19
  608.1 11.2 slice-start.20
  629.7 233.0 %all-to-all-start.3 = ((bf16[4,4,1152]{2,0,1:T(4,128)(2,1)}), bf16[4,4,1152]{2,0,1:T(4,128)(2,1)S(1)}, u32[]{:S(2)}, u32[]{:S(2)}) async-start(bf16[4,4,1152]{2,0,1:T(4,128)(2,1)} %bitcast.52), calls=%async_computation.3 | async-start | bytes 73728 | tf_op jit(solution)/shard_map/all_to_all | solution.py:223
  633.0 268.2 %all-reduce.27.cloned.1.call-start = ((), (), s32[]{:S(2)}) async-start(), calls=%async_computation.11 | async-start | bytes 188416 | tf_op jit(solution)/shard_map/psum | solution.py:242
  633.2 15.9 slice-start.12
  638.7 10.4 slice-start.13
  649.9 14.2 slice-start.15
  850.5 10.9 copy-start.99
  850.5 10.9 copy-start.100
  850.5 11.5 copy-start.91
  850.5 11.5 copy-start.93
  859.5 32.0 %copy-start.81 = (bf16[8,768]{1,0:T(8,128)(2,1)S(1)}, bf16[8,768]{1,0:T(8,128)(2,1)}, u32[]{:S(2)}) copy-start(bf16[8,768]{1,0:T(8,128)(2,1)} %copy-done.80) | copy-start | bytes 36868
  859.5 32.0 %copy-start.83 = (bf16[8,768]{1,0:T(8,128)(2,1)S(1)}, bf16[8,768]{1,0:T(8,128)(2,1)}, u32[]{:S(2)}) copy-start(bf16[8,768]{1,0:T(8,128)(2,1)} %copy-done.82) | copy-start | bytes 36868
  859.5 32.0 %copy-start.114 = (s32[8]{0:T(128)S(1)}, s32[8]{0:T(128)}, u32[]{:S(2)}) copy-start(s32[8]{0:T(128)} %eq.102) | copy-start | bytes 100
  862.6 10.8 all-to-all-start.2
  867.7 1177.6 %all-reduce.29.cloned.1.call-start = ((), (), s32[]{:S(2)}) async-start(), calls=%async_computation.12 | async-start | bytes 68911104 | tf_op jit(solution)/shard_map/psum | solution.py:242
  867.7 27.0 %copy-start.113 = (s32[8]{0:T(128)S(1)}, s32[8]{0:T(128)}, u32[]{:S(2)}) copy-start(s32[8]{0:T(128)} %eq.106) | copy-start | bytes 100
  897.9 1203.2 %all-reduce.23.cloned.1.call-start = ((), (), s32[]{:S(2)}) async-start(), calls=%async_computation.9 | async-start | bytes 188416 | tf_op jit(solution)/shard_map/psum | solution.py:241
  901.2 1264.3 %all-reduce.21.cloned.1.call-start = ((), (), s32[]{:S(2)}) async-start(), calls=%async_computation.8 | async-start | bytes 3538944 | tf_op jit(solution)/shard_map/psum | solution.py:269
  905.1 1678.6 %all-reduce.25.cloned.1.call-start = ((), (), s32[]{:S(2)}) async-start(), calls=%async_computation.10 | async-start | bytes 68911104 | tf_op jit(solution)/shard_map/psum | solution.py:241
  (93 other events, 411.7 us)
Sparse Core Ops, SparseCore 0:
  9.7 75.3 all-gather.9
  86.7 29.2 all-gather.11
  117.5 88.5 all-gather.13
  207.5 90.2 all-gather.15
  862.8 35.9 all-reduce.26
  902.8 1142.4 all-reduce.28
  2049.4 51.6 all-reduce.22
  2105.0 60.4 all-reduce.20
  2171.0 412.6 all-reduce.24
